TPU v7x, 32 devices: a whole 2x2x4 slice. The times are simulated.
32 devices in a mesh: grp: 4 (over x, core), box: 8 (over z, y).
Axes of the slice: x: 2, y: 2, z: 4, core: 2. Of those that a mesh axis runs over, the one named last changes fastest.
Arguments:
- source_field: float32 [128, 256, 128], P('grp', 'box'), may hold values from -7 to 7
- region_tags: int32 [128, 256, 128], P('grp', 'box'), may hold values from 0 to 7
- region_coef: float32 [8], replicated, may hold values from 0.2 to 5
- roughness: float32 [128, 256, 128], P('grp', 'box'), may hold values from 0.5 to 2
Outputs:
- solution: float32 [128, 256, 128], P('grp', 'box')
- residual: float32 [128, 256, 128], P('grp', 'box')
All inputs are finite; a program needn't handle non-finite values.
Results may differ from a plain program's by a relative error of at most 0.0003.
Values sent between devices are 32-bit elements; how exact they have to be, the bound alone decides.
A program may use at most 192 MiB of HBM per device.

v0:
```python
import jax
import jax.numpy as jnp
from jax import lax
from jax.sharding import PartitionSpec as P

LEVELS = 5
NU = 2
NB = 4
CYCLES = 2


relax_weight = 0.8


def padded_2(x, sides, width):
    for axis, dim in sides:
        size, length = (lax.axis_size(axis), x.shape[dim])
        up = [(i, (i + 1) % size) for i in range(size - 1)]
        down = [(j, i) for i, j in up]
        last = lax.slice_in_dim(x, length - width, length, axis=dim)
        first = lax.slice_in_dim(x, 0, width, axis=dim)
        before = lax.ppermute(last, axis, up)
        after = lax.ppermute(first, axis, down)
        x = jnp.concatenate([before, x, after], axis=dim)
    return x


def coarsen(values):
    size_x, size_y, size_z = values.shape
    return values.reshape(size_x // 2, 2, size_y // 2, 2, size_z // 2, 2).sum(axis=(1, 3, 5))


def refine(values):
    return jnp.repeat(jnp.repeat(jnp.repeat(values, 2, 0), 2, 1), 2, 2)


def neighbours(padded):
    return [
        padded[2:, 1:-1, 1:-1],
        padded[:-2, 1:-1, 1:-1],
        padded[1:-1, 2:, 1:-1],
        padded[1:-1, :-2, 1:-1],
        padded[1:-1, 1:-1, 2:],
        padded[1:-1, 1:-1, :-2],
    ]


def weights_of(coef_padded):
    center = coef_padded[1:-1, 1:-1, 1:-1]
    face_weights = [(center + other) * 0.5 for other in neighbours(coef_padded)]
    diag_sum = face_weights[0]
    for other in face_weights[1:]:
        diag_sum = diag_sum + other
    return (face_weights, diag_sum)


def apply_padded(values, padded, face_weights, diag_sum):
    near = neighbours(padded)
    total = face_weights[0] * near[0]
    for index in range(1, 6):
        total = total + face_weights[index] * near[index]
    return diag_sum * values - total


def pad_depth(values):
    return jnp.pad(values, ((0, 0), (0, 0), (1, 1)))


def rim_cells(values):
    extended = padded_2(values, (("grp", 0), ("box", 1)), 1)
    return pad_depth(extended)


def coef_padded(values):
    return padded_2(values, (("grp", 0), ("box", 1)), 1)


def gather_box(pieces):
    return (
        lax.all_gather(pieces[0], "box", axis=1, tiled=True),
        lax.all_gather(pieces[1], "box", axis=1, tiled=True),
    )


def slab_rims(values):
    extended = padded_2(values, (("grp", 0),), 1)
    return jnp.pad(extended, ((0, 0), (1, 1), (1, 1)))


def group_total(value):
    return lax.psum(value, "grp")


def smooth(values, source, face_weights, diag_sum, count, padder):
    for sweep_index in range(count):
        result = apply_padded(values, padder(values), face_weights, diag_sum)
        values = values + relax_weight * (source - result) / diag_sum
    return values


def krylov_solve(source, face_weights, diag_sum, padder, totaler):
    values = jnp.zeros_like(source)
    remain = source
    direction = source
    norm_now = totaler(jnp.sum(remain * remain))
    for step_index in range(NB):
        image = apply_padded(direction, padder(direction), face_weights, diag_sum)
        alpha = norm_now / totaler(jnp.sum(direction * image))
        values = values + alpha * direction
        remain = remain - alpha * image
        norm_next = totaler(jnp.sum(remain * remain))
        direction = remain + norm_next / norm_now * direction
        norm_now = norm_next
    return values


def level_smooth(values, source, level_ops, count):
    return smooth(values, source, level_ops[0], level_ops[1], count, rim_cells)


def v_cycle(level_index, values, source, operators, bottom):
    if level_index == LEVELS - 1:
        return bottom(source)
    level_ops = operators[level_index]
    values = level_smooth(values, source, level_ops, NU)
    remain = source - apply_padded(values, rim_cells(values), level_ops[0], level_ops[1])
    coarse_source = 0.5 * coarsen(remain)
    correction = v_cycle(
        level_index + 1, jnp.zeros_like(coarse_source), coarse_source, operators, bottom
    )
    values = values + refine(correction)
    return level_smooth(values, source, level_ops, NU)


def body(source_field, region_tags, region_coef, roughness):
    coefficient = jnp.zeros(source_field.shape, jnp.float32)
    for region in range(region_coef.shape[0]):
        coefficient = coefficient + jnp.where(
            region_tags == region, region_coef[region], jnp.float32(0.0)
        )
    coefficient = coefficient * roughness
    fields = [coefficient]
    for level_index in range(1, LEVELS):
        fields.append(coarsen(fields[-1]) * 0.125)
    operators = []
    for level_index in range(LEVELS - 1):
        field = fields[level_index]
        extended = coef_padded(field)
        face_int, diag_int = weights_of(pad_depth(extended))
        operators.append((face_int, diag_int, None, None, None))
    coarsest = fields[-1]
    coarse_x, coarse_y, coarse_z = coarsest.shape
    coarse_ext = coef_padded(coarsest)
    x_padded = coarse_ext[:, 1:-1, :]

    def bottom(source):
        slab_source, slab_coef = gather_box((source, x_padded))
        slab_w, slab_d = weights_of(jnp.pad(slab_coef, ((0, 0), (1, 1), (1, 1))))
        slab_field = krylov_solve(slab_source, slab_w, slab_d, slab_rims, group_total)
        return lax.dynamic_slice_in_dim(slab_field, lax.axis_index("box") * coarse_y, coarse_y, 1)

    solution = jnp.zeros_like(source_field)
    for cycle_index in range(CYCLES):
        solution = v_cycle(0, solution, source_field, operators, bottom)
    fine_ops = operators[0]
    residual = source_field - apply_padded(solution, rim_cells(solution), fine_ops[0], fine_ops[1])
    return (solution, residual)


def solution(mesh):
    return jax.shard_map(
        body,
        mesh=mesh,
        in_specs=(P("grp", "box", None), P("grp", "box", None), P(), P("grp", "box", None)),
        out_specs=(P("grp", "box", None), P("grp", "box", None)),
        check_vma=False,
    )
```

profile of v0, /device:TPU:0, one launch (start us, length us, event | category | flops | bytes accessed | tf_op | source)
XLA Modules:
  0.0 1490.3 jit_solution(8975298969838905094)
XLA Ops:
  18.5 8.8 add_multiply_fusion
  33.8 34.9 %reshape.116 = f32[16,2,16,2,64,2]{5,4,3,2,1,0:T(8,128)} reshape(f32[32,32,128]{2,1,0:T(8,128)S(1)} %copy.1346) | data formatting | bytes 1048576 | tf_op jit(solution)/shard_map/reshape | solution.py:30
  68.7 12.2 reduce_sum.253
  155.2 10.9 fusion.10
  213.3 11.5 fusion.134
  266.4 12.8 fusion.120
  282.7 35.6 %reshape.115 = f32[16,2,16,2,64,2]{5,4,3,2,1,0:T(8,128)} reshape(f32[32,32,128]{2,1,0:T(8,128)} %copy.1345) | data formatting | bytes 1048576 | tf_op jit(solution)/shard_map/reshape | solution.py:30
  318.4 12.2 reduce_sum.252
  471.2 32.2 %all_gather.11 = f32[4,16,8]{2,0,1:T(4,128)S(1)} all-gather(f32[4,2,8]{2,0,1:T(4,128)S(1)} %copy.1348), channel_id=1, replica_groups=mesh['grp'=4,'box'=8] {'box'}, dimensions={1}, use_global_device_ids=true | all-gather | bytes 2304 | tf_op jit(solution)/shard_map/all_gather | solution.py:81
  503.8 26.0 %all_gather.10 = f32[2,16,8]{2,0,1:T(2,128)S(1)} all-gather(f32[2,2,8]{2,0,1:T(2,128)S(1)} %copy.1347), channel_id=1, replica_groups=mesh['grp'=4,'box'=8] {'box'}, dimensions={1}, use_global_device_ids=true | all-gather | bytes 1152 | tf_op jit(solution)/shard_map/all_gather | solution.py:80
  537.5 8.6 all-reduce.60
  562.8 8.6 psum.115
  766.0 14.7 fusion.109
  816.8 11.5 fusion.95
  862.4 11.5 fusion.81
  908.1 11.5 fusion.67
  952.9 12.8 fusion.53
  969.1 35.6 %reshape.132 = f32[16,2,16,2,64,2]{5,4,3,2,1,0:T(8,128)} reshape(f32[32,32,128]{2,1,0:T(8,128)} %copy.1409) | data formatting | bytes 1048576 | tf_op jit(solution)/shard_map/reshape | solution.py:30
  1004.8 12.3 reduce_sum.268
  1123.9 26.0 %all_gather.12 = f32[2,16,8]{2,0,1:T(2,128)S(1)} all-gather(f32[2,2,8]{2,0,1:T(2,128)S(1)} %copy.1410), channel_id=1, replica_groups=mesh['grp'=4,'box'=8] {'box'}, dimensions={1}, use_global_device_ids=true | all-gather | bytes 1152 | tf_op jit(solution)/shard_map/all_gather | solution.py:80
  1157.7 8.6 all-reduce.59
  1378.6 13.2 fusion.42
  1428.0 11.5 fusion.28
  1474.5 12.1 fusion.14
  (920 shorter events, 1070.6 us)
Async XLA Ops:
  0.7 90.8 %collective-permute-start.5 = (f32[1,32,128]{1,0,2:T(1,128)S(1)}, f32[1,32,128]{1,0,2:T(1,128)S(1)}, u32[]{:S(2)}, u32[]{:S(2)}) collective-permute-start(f32[1,32,128]{1,0,2:T(1,128)S(1)} %broadcast.179), channel_id=1, source_target_pairs={{0,8},{8,16},{16,24},{1,9},{9,17},{17,25},{2,10},{10,18},{18,26},{... | collective-permute-start | bytes 49160 | tf_op jit(solution)/shard_map/ppermute | solution.py:22
  3.2 88.3 %collective-permute-start.4 = (f32[1,32,128]{1,0,2:T(1,128)S(1)}, f32[1,32,128]{1,0,2:T(1,128)S(1)}, u32[]{:S(2)}, u32[]{:S(2)}) collective-permute-start(f32[1,32,128]{1,0,2:T(1,128)S(1)} %broadcast.179), channel_id=1, source_target_pairs={{8,0},{16,8},{24,16},{9,1},{17,9},{25,17},{10,2},{18,10},{26,18},{... | collective-permute-start | bytes 49160 | tf_op jit(solution)/shard_map/ppermute | solution.py:23
  5.0 390.1 %collective-permute-start.53 = (f32[1,4,16]{2,1,0:T(4,128)}, f32[1,4,16]{2,1,0:T(4,128)S(1)}, u32[]{:S(2)}, u32[]{:S(2)}) collective-permute-start(f32[1,4,16]{2,1,0:T(4,128)} %broadcast.191), channel_id=1, source_target_pairs={{0,8},{8,16},{16,24},{1,9},{9,17},{17,25},{2,10},{10,18},{18,26},{... | collective-permute-start | bytes 776 | tf_op jit(solution)/shard_map/ppermute | solution.py:22
  27.4 80.0 %collective-permute-start.1 = (f32[1,32,128]{1,0,2:T(1,128)S(1)}, f32[1,32,128]{1,0,2:T(1,128)S(1)}, u32[]{:S(2)}, u32[]{:S(2)}) collective-permute-start(f32[1,32,128]{1,0,2:T(1,128)S(1)} %get-tuple-element.106), channel_id=1, source_target_pairs={{0,8},{8,16},{16,24},{1,9},{9,17},{17,25},{2,10},{10,18},{18,26},{... | collective-permute-start | bytes 49160 | tf_op jit(solution)/shard_map/ppermute | solution.py:22
  31.0 76.4 %collective-permute-start = (f32[1,32,128]{1,0,2:T(1,128)S(1)}, f32[1,32,128]{1,0,2:T(1,128)S(1)}, u32[]{:S(2)}, u32[]{:S(2)}) collective-permute-start(f32[1,32,128]{1,0,2:T(1,128)S(1)} %get-tuple-element.107), channel_id=1, source_target_pairs={{8,0},{16,8},{24,16},{9,1},{17,9},{25,17},{10,2},{18,10},{26,18},{... | collective-permute-start | bytes 49160 | tf_op jit(solution)/shard_map/ppermute | solution.py:23
  101.5 29.4 %collective-permute-start.6 = (f32[34,1,128]{2,1,0:T(1,128)S(1)}, f32[34,1,128]{2,1,0:T(1,128)S(1)}, u32[]{:S(2)}, u32[]{:S(2)}) collective-permute-start(f32[34,1,128]{2,1,0:T(1,128)S(1)} %copy.1324), channel_id=1, source_target_pairs={{1,0},{2,1},{3,2},{4,3},{5,4},{6,5},{7,6},{9,8},{10,9},{11,10},{12... | collective-permute-start | bytes 52232 | tf_op jit(solution)/shard_map/ppermute | solution.py:23
  102.8 24.5 %collective-permute-start.7 = (f32[34,1,128]{2,1,0:T(1,128)S(1)}, f32[34,1,128]{2,1,0:T(1,128)S(1)}, u32[]{:S(2)}, u32[]{:S(2)}) collective-permute-start(f32[34,1,128]{2,1,0:T(1,128)S(1)} %copy.1326), channel_id=1, source_target_pairs={{0,1},{1,2},{2,3},{3,4},{4,5},{5,6},{6,7},{8,9},{9,10},{10,11},{11... | collective-permute-start | bytes 52232 | tf_op jit(solution)/shard_map/ppermute | solution.py:22
  115.9 26.9 %collective-permute-start.2 = (f32[34,1,128]{2,1,0:T(1,128)S(1)}, f32[34,1,128]{2,1,0:T(1,128)S(1)}, u32[]{:S(2)}, u32[]{:S(2)}) collective-permute-start(f32[34,1,128]{2,1,0:T(1,128)S(1)} %copy.1318), channel_id=1, source_target_pairs={{1,0},{2,1},{3,2},{4,3},{5,4},{6,5},{7,6},{9,8},{10,9},{11,10},{12... | collective-permute-start | bytes 52232 | tf_op jit(solution)/shard_map/ppermute | solution.py:23
  117.2 19.5 %collective-permute-start.3 = (f32[34,1,128]{2,1,0:T(1,128)S(1)}, f32[34,1,128]{2,1,0:T(1,128)S(1)}, u32[]{:S(2)}, u32[]{:S(2)}) collective-permute-start(f32[34,1,128]{2,1,0:T(1,128)S(1)} %copy.1320), channel_id=1, source_target_pairs={{0,1},{1,2},{2,3},{3,4},{4,5},{5,6},{6,7},{8,9},{9,10},{10,11},{11... | collective-permute-start | bytes 52232 | tf_op jit(solution)/shard_map/ppermute | solution.py:22
  127.3 269.2 %collective-permute-start.52 = (f32[1,4,16]{2,1,0:T(4,128)}, f32[1,4,16]{2,1,0:T(4,128)S(1)}, u32[]{:S(2)}, u32[]{:S(2)}) collective-permute-start(f32[1,4,16]{2,1,0:T(4,128)} %broadcast.191), channel_id=1, source_target_pairs={{8,0},{16,8},{24,16},{9,1},{17,9},{25,17},{10,2},{18,10},{26,18},{... | collective-permute-start | bytes 776 | tf_op jit(solution)/shard_map/ppermute | solution.py:23
  130.9 56.6 %collective-permute-start.21 = (f32[1,16,64]{2,1,0:T(8,128)S(1)}, f32[1,16,64]{2,1,0:T(8,128)S(1)}, u32[]{:S(2)}, u32[]{:S(2)}) collective-permute-start(f32[1,16,64]{2,1,0:T(8,128)S(1)} %broadcast.183), channel_id=1, source_target_pairs={{0,8},{8,16},{16,24},{1,9},{9,17},{17,25},{2,10},{10,18},{18,26},{... | collective-permute-start | bytes 12296 | tf_op jit(solution)/shard_map/ppermute | solution.py:22
  136.7 29.6 %collective-permute-start.17 = (f32[1,16,64]{2,1,0:T(8,128)S(1)}, f32[1,16,64]{2,1,0:T(8,128)S(1)}, u32[]{:S(2)}, u32[]{:S(2)}) collective-permute-start(f32[1,16,64]{2,1,0:T(8,128)S(1)} %get-tuple-element.144), channel_id=1, source_target_pairs={{0,8},{8,16},{16,24},{1,9},{9,17},{17,25},{2,10},{10,18},{18,26},{... | collective-permute-start | bytes 12296 | tf_op jit(solution)/shard_map/ppermute | solution.py:22
  142.7 26.6 %collective-permute-start.16 = (f32[1,16,64]{2,1,0:T(8,128)S(1)}, f32[1,16,64]{2,1,0:T(8,128)S(1)}, u32[]{:S(2)}, u32[]{:S(2)}) collective-permute-start(f32[1,16,64]{2,1,0:T(8,128)S(1)} %get-tuple-element.145), channel_id=1, source_target_pairs={{8,0},{16,8},{24,16},{9,1},{17,9},{25,17},{10,2},{18,10},{26,18},{... | collective-permute-start | bytes 12296 | tf_op jit(solution)/shard_map/ppermute | solution.py:23
  174.3 168.8 %collective-permute-start.37 = (f32[1,8,32]{2,1,0:T(8,128)}, f32[1,8,32]{2,1,0:T(8,128)S(1)}, u32[]{:S(2)}, u32[]{:S(2)}) collective-permute-start(f32[1,8,32]{2,1,0:T(8,128)} %broadcast.187), channel_id=1, source_target_pairs={{0,8},{8,16},{16,24},{1,9},{9,17},{17,25},{2,10},{10,18},{18,26},{... | collective-permute-start | bytes 3080 | tf_op jit(solution)/shard_map/ppermute | solution.py:22
  195.8 29.1 %collective-permute-start.23 = (f32[18,1,64]{2,1,0:T(1,128)S(1)}, f32[18,1,64]{2,1,0:T(1,128)S(1)}, u32[]{:S(2)}, u32[]{:S(2)}) collective-permute-start(f32[18,1,64]{2,1,0:T(1,128)S(1)} %get-tuple-element.126), channel_id=1, source_target_pairs={{0,1},{1,2},{2,3},{3,4},{4,5},{5,6},{6,7},{8,9},{9,10},{10,11},{11... | collective-permute-start | bytes 13832 | tf_op jit(solution)/shard_map/ppermute | solution.py:22
  202.9 23.4 %collective-permute-start.22 = (f32[18,1,64]{2,1,0:T(1,128)S(1)}, f32[18,1,64]{2,1,0:T(1,128)S(1)}, u32[]{:S(2)}, u32[]{:S(2)}) collective-permute-start(f32[18,1,64]{2,1,0:T(1,128)S(1)} %get-tuple-element.127), channel_id=1, source_target_pairs={{1,0},{2,1},{3,2},{4,3},{5,4},{6,5},{7,6},{9,8},{10,9},{11,10},{12... | collective-permute-start | bytes 13832 | tf_op jit(solution)/shard_map/ppermute | solution.py:23
  252.1 79.9 %collective-permute-start.33 = (f32[1,8,32]{2,1,0:T(8,128)S(1)}, f32[1,8,32]{2,1,0:T(8,128)S(1)}, u32[]{:S(2)}, u32[]{:S(2)}) collective-permute-start(f32[1,8,32]{2,1,0:T(8,128)S(1)} %get-tuple-element.182), channel_id=1, source_target_pairs={{0,8},{8,16},{16,24},{1,9},{9,17},{17,25},{2,10},{10,18},{18,26},{... | collective-permute-start | bytes 3080 | tf_op jit(solution)/shard_map/ppermute | solution.py:22
  257.0 80.4 %collective-permute-start.32 = (f32[1,8,32]{2,1,0:T(8,128)S(1)}, f32[1,8,32]{2,1,0:T(8,128)S(1)}, u32[]{:S(2)}, u32[]{:S(2)}) collective-permute-start(f32[1,8,32]{2,1,0:T(8,128)S(1)} %get-tuple-element.183), channel_id=1, source_target_pairs={{8,0},{16,8},{24,16},{9,1},{17,9},{25,17},{10,2},{18,10},{26,18},{... | collective-permute-start | bytes 3080 | tf_op jit(solution)/shard_map/ppermute | solution.py:23
  341.7 67.5 %collective-permute-start.48 = (f32[1,4,16]{2,1,0:T(4,128)}, f32[1,4,16]{2,1,0:T(4,128)S(1)}, u32[]{:S(2)}, u32[]{:S(2)}) collective-permute-start(f32[1,4,16]{2,1,0:T(4,128)} %get-tuple-element.236), channel_id=1, source_target_pairs={{8,0},{16,8},{24,16},{9,1},{17,9},{25,17},{10,2},{18,10},{26,18},{... | collective-permute-start | bytes 776 | tf_op jit(solution)/shard_map/ppermute | solution.py:23
  376.4 34.1 %collective-permute-start.49 = (f32[1,4,16]{2,1,0:T(4,128)}, f32[1,4,16]{2,1,0:T(4,128)S(1)}, u32[]{:S(2)}, u32[]{:S(2)}) collective-permute-start(f32[1,4,16]{2,1,0:T(4,128)} %get-tuple-element.237), channel_id=1, source_target_pairs={{0,8},{8,16},{16,24},{1,9},{9,17},{17,25},{2,10},{10,18},{18,26},{... | collective-permute-start | bytes 776 | tf_op jit(solution)/shard_map/ppermute | solution.py:22
  396.5 23.0 %collective-permute-start.55 = (f32[6,1,16]{2,1,0:T(1,128)S(1)}, f32[6,1,16]{2,1,0:T(1,128)S(1)}, u32[]{:S(2)}, u32[]{:S(2)}) collective-permute-start(f32[6,1,16]{2,1,0:T(1,128)S(1)} %get-tuple-element.202), channel_id=1, source_target_pairs={{0,1},{1,2},{2,3},{3,4},{4,5},{5,6},{6,7},{8,9},{9,10},{10,11},{11... | collective-permute-start | bytes 1160 | tf_op jit(solution)/shard_map/ppermute | solution.py:22
  410.5 20.7 %collective-permute-start.51 = (f32[6,1,16]{2,1,0:T(1,128)S(1)}, f32[6,1,16]{2,1,0:T(1,128)S(1)}, u32[]{:S(2)}, u32[]{:S(2)}) collective-permute-start(f32[6,1,16]{2,1,0:T(1,128)S(1)} %get-tuple-element.200), channel_id=1, source_target_pairs={{0,1},{1,2},{2,3},{3,4},{4,5},{5,6},{6,7},{8,9},{9,10},{10,11},{11... | collective-permute-start | bytes 1160 | tf_op jit(solution)/shard_map/ppermute | solution.py:22
  465.3 38.1 %collective-permute-start.63 = (f32[6,1,16]{2,1,0:T(1,128)S(1)}, f32[6,1,16]{2,1,0:T(1,128)S(1)}, u32[]{:S(2)}, u32[]{:S(2)}) collective-permute-start(f32[6,1,16]{2,1,0:T(1,128)S(1)} %get-tuple-element.196), channel_id=1, source_target_pairs={{0,1},{1,2},{2,3},{3,4},{4,5},{5,6},{6,7},{8,9},{9,10},{10,11},{11... | collective-permute-start | bytes 1160 | tf_op jit(solution)/shard_map/ppermute | solution.py:22
  469.9 33.6 %collective-permute-start.62 = (f32[6,1,16]{2,1,0:T(1,128)S(1)}, f32[6,1,16]{2,1,0:T(1,128)S(1)}, u32[]{:S(2)}, u32[]{:S(2)}) collective-permute-start(f32[6,1,16]{2,1,0:T(1,128)S(1)} %get-tuple-element.197), channel_id=1, source_target_pairs={{1,0},{2,1},{3,2},{4,3},{5,4},{6,5},{7,6},{9,8},{10,9},{11,10},{12... | collective-permute-start | bytes 1160 | tf_op jit(solution)/shard_map/ppermute | solution.py:23
  (254 other events, 2790.5 us)
where the time goes:
time: 1500 us; the launch traced here: 1490 us
  starting transfers between devices  439 us (29%)
  local copies, waits for them, and re-layouts  331 us (22%)
  other arithmetic  300 us (20%)
  waiting for transfers between devices  206 us (14%)
  blocking collectives  191 us (13%)
  between operations  23.8 us (2%)
    ppermute x93, starting transfers between devices, padded_2(): before = lax.ppermute(last, axis, up)  316 us
    ppermute x93, waiting for transfers between devices, padded_2(): after = lax.ppermute(first, axis, down)  203 us
    ppermute x93, starting transfers between devices, padded_2(): after = lax.ppermute(first, axis, down)  123 us
    reshape x9, local copies, waits for them, and re-layouts, coarsen(): values.reshape(size_x // 2, 2, size_y // 2, 2, size_z // 2, 2)  120 us
    psum x14, blocking collectives, group_total(): return lax.psum(value, 'grp')  107 us
    add x25, other arithmetic, smooth(): values = values + relax_weight * (source - result) / diag_sum  88.1 us
    concatenate x93, other arithmetic, padded_2(): x = jnp.concatenate([before, x, after], axis=dim)  84.2 us
    slice x70, local copies, waits for them, and re-layouts, padded_2(): last = lax.slice_in_dim(x, length - width, length, axis=dim)  69.9 us
  transfers between devices with their start and end apart: 186, of which 74 were waited for; matrix products, arithmetic and copies ran while one was open for 20% of the time, Pallas kernels for 0%

commit v1 on v0

v1 whole, which is shorter than its diff:
```python
import functools
import jax
import jax.numpy as jnp
from jax import lax
from jax.experimental import pallas as pl
from jax.experimental.pallas import tpu as pltpu
from jax.sharding import PartitionSpec as P

NB = 4
LANES = 128
HX = 8
YO = 16
GX = 4
GY = 8
DIRECTIONS = [(dx, dy) for dx in (-1, 0, 1) for dy in (-1, 0, 1) if (dx, dy) != (0, 0)]


class Level:
    def __init__(self, shift, nx, ny, x0, y0, ylo, yhi, refs):
        self.shift, self.nx, self.ny, self.x0, self.y0 = shift, nx, ny, x0, y0
        self.ylo, self.yhi = ylo, yhi
        self.C, self.WL, self.WH, self.G, self.D, self.VA, self.VB = refs


def lane_index(shape):
    return lax.broadcasted_iota(jnp.int32, shape, len(shape) - 1)


def roll(values, shift):
    return pltpu.roll(values, shift % LANES, values.ndim - 1)


def pair_sum(values, shift):
    even = (lane_index(values.shape) // shift) % 2 == 0
    return values + jnp.where(even, roll(values, LANES - shift), roll(values, shift))


def off_diagonal(L, V, x, n, y, rows):
    block = V[pl.ds(x - 1, n + 2), pl.ds(y, rows), :]
    coef = L.C[pl.ds(x - 1, n + 2), pl.ds(y, rows), :]
    flow = block * coef
    center, near = block[1:-1], coef[1:-1]
    v_down = V[pl.ds(x, n), pl.ds(y - 1, rows), :]
    v_up = V[pl.ds(x, n), pl.ds(y + 1, rows), :]
    c_down = L.C[pl.ds(x, n), pl.ds(y - 1, rows), :]
    c_up = L.C[pl.ds(x, n), pl.ds(y + 1, rows), :]
    total = (block[:-2] + block[2:]) + (v_down + v_up)
    total = near * total + (flow[:-2] + flow[2:]) + (c_down * v_down + c_up * v_up)
    total = total + L.WL[pl.ds(x, n), pl.ds(y, rows), :] * roll(center, L.shift)
    total = total + L.WH[pl.ds(x, n), pl.ds(y, rows), :] * roll(center, LANES - L.shift)
    return center, total


def each_x(start, count, step, body):
    def run(i, carry):
        body(start + i * step, i)
        return carry

    lax.fori_loop(0, count // step, run, 0)


def tiles(lo, hi):
    return range(lo, hi, 8)


def operators(L, k):
    def body(x, i):
        for y in tiles(L.ylo, L.yhi):
            at = (pl.ds(x, 2), pl.ds(y, 8), slice(None))
            coef = L.C[pl.ds(x - 1, 4), pl.ds(y, 8), :]
            c = coef[1:-1]
            lane = lane_index(c.shape)
            down = jnp.where(lane < L.shift, 0.0, roll(c, L.shift))
            up = jnp.where(lane >= LANES - L.shift, 0.0, roll(c, LANES - L.shift))
            L.WL[at] = jnp.where(lane < L.shift, 0.0, c + down)
            L.WH[at] = jnp.where(lane >= LANES - L.shift, 0.0, c + up)
            diag = 6.0 * c + (coef[:-2] + coef[2:]) + (down + up)
            diag = diag + (L.C[pl.ds(x, 2), pl.ds(y - 1, 8), :] + L.C[pl.ds(x, 2), pl.ds(y + 1, 8), :])
            L.D[at] = diag
            L.G[at] = jnp.where(c > 0.0, 0.8 / jnp.where(c > 0.0, diag, 1.0), 0.0)

    each_x(L.x0 - k, L.nx + 2 * k, 2, body)


def first_sweep(L, F, dst, k):
    def body(x, i):
        for y in tiles(L.ylo, L.yhi):
            at = (pl.ds(x, 2), pl.ds(y, 8), slice(None))
            dst[at] = L.G[at] * F[at]

    each_x(L.x0 - k, L.nx + 2 * k, 2, body)


def sweep(L, F, src, dst, k):
    def body(x, i):
        for y in tiles(L.ylo, L.yhi):
            at = (pl.ds(x, 2), pl.ds(y, 8), slice(None))
            center, total = off_diagonal(L, src, x, 2, y, 8)
            dst[at] = 0.2 * center + L.G[at] * (F[at] + total)

    each_x(L.x0 - k, L.nx + 2 * k, 2, body)


def residual_pairs(L, F, V, R):
    def body(x, i):
        for y in tiles(L.y0, L.y0 + L.ny):
            at = (pl.ds(x, 2), pl.ds(y, 8), slice(None))
            center, total = off_diagonal(L, V, x, 2, y, 8)
            left = F[at] - L.D[at] * center + total
            R[i, pl.ds(y - L.y0, 8), :] = left[0] + left[1]

    each_x(L.x0, L.nx, 2, body)


def coef_pairs(L, R):
    def body(x, i):
        for y in tiles(L.y0, L.y0 + L.ny):
            c = L.C[pl.ds(x, 2), pl.ds(y, 8), :]
            R[i, pl.ds(y - L.y0, 8), :] = c[0] + c[1]

    each_x(L.x0, L.nx, 2, body)


def coarse_row(L, R, i, factor):
    half = L.ny // 2
    rows = R[i, pl.ds(0, half, stride=2), :] + R[i, pl.ds(1, half, stride=2), :]
    return pair_sum(rows, L.shift) * factor


def coarse_rows(L, R, factor, dst, x0, y0):
    def body(i, _):
        dst[x0 + i, pl.ds(y0, L.ny // 2), :] = coarse_row(L, R, i, factor)

    each_x(0, L.nx // 2, 1, body)


def packed(L, R, factor):
    count = L.nx // 2
    rows = [coarse_row(L, R, i, factor) for i in range(count)]
    which = lane_index(rows[0].shape) % count
    out = rows[0]
    for i in range(1, count):
        out = jnp.where(which == i, rows[i], out)
    return out


def unpack(slots, flat, dst, ng, nb, tx, ty):
    def body(g, _):
        for b in range(nb):
            flat[pl.ds(b * ty, ty), :] = slots[g * nb + b]
        for y in tiles(0, nb * ty):
            rows = flat[pl.ds(y, 8), :]
            rolled = {d: roll(rows, d) for d in range(1 - tx, tx)}
            which = lane_index(rows.shape) % tx
            for i in range(tx):
                out = rolled[-i]
                for d in range(1, tx):
                    out = jnp.where(which == d, rolled[d - i], out)
                dst[GX + g * tx + i, pl.ds(GY + y, 8), :] = out

    each_x(0, ng, 1, body)


def add_refined(L, src, dst, E, ex, ey, k):
    half = (L.yhi - L.ylo) // 2

    def body(x, i):
        e = E[ex + i, pl.ds(ey, half), :]
        for dx in range(2):
            for phase in range(2):
                at = (x + dx, pl.ds(L.ylo + phase, half, stride=2), slice(None))
                dst[at] = src[at] + e

    each_x(L.x0 - k, L.nx + 2 * k, 2, body)


def total_of(values):
    return jnp.sum(values, axis=(0, 1, 2), keepdims=True)


def krylov(L, F, E, V):
    at = (pl.ds(L.x0, L.nx), pl.ds(L.y0, L.ny), slice(None))
    remain = F[at]
    direction = remain
    values = jnp.zeros_like(remain)
    norm_now = total_of(remain * remain)
    for step in range(NB):
        V[at] = direction
        _, total = off_diagonal(L, V, L.x0, L.nx, L.y0, L.ny)
        image = L.D[at] * direction - total
        alpha = norm_now / total_of(direction * image)
        values = values + alpha * direction
        if step < NB - 1:
            remain = remain - alpha * image
            norm_next = total_of(remain * remain)
            direction = remain + (norm_next / norm_now) * direction
            norm_now = norm_next
    E[at] = values


def zero(ref):
    def body(i, _):
        ref[i] = jnp.zeros(ref.shape[1:], ref.dtype)

    each_x(0, ref.shape[0], 1, body)


def kernel(ng, nb, source, tags, coef, rough, out_v, out_r, *scratch):
    scratch = list(scratch)

    def take(count):
        taken = scratch[:count]
        del scratch[:count]
        return taken

    nx, ny = source.shape[0], source.shape[1]
    L = []
    for l in range(3):
        L.append(Level(1 << l, nx >> l, ny >> l, HX, YO, 8, (ny >> l) + 24, take(7)))
    tx, ty = nx >> 3, ny >> 3
    L.append(Level(8, ng * tx, nb * ty, GX, GY, GY, GY + nb * ty, take(7)))
    L.append(Level(16, ng * tx // 2, nb * ty // 2, 2, GY, GY, GY + nb * ty // 2, take(7)))
    f0, f1a, f1b, f2a, f2b, f3, f4, kept = take(8)
    f1, f2 = (f1a, f1b), (f2a, f2b)
    R0, R1, R2, R3, flat = take(5)
    slots = take(3)
    halo_send, halo_recv, all_send, all_recv = take(4)

    g, b = lax.axis_index("grp"), lax.axis_index("box")
    me = g * nb + b
    count = ng * nb

    for ref in [f0, f1a, f1b, f2a, f2b, kept]:
        zero(ref)
    for level in L:
        zero(level.C)
        zero(level.VA)
        zero(level.VB)

    barrier = pltpu.get_barrier_semaphore()

    def others(body):
        def run(i, carry):
            other = lax.rem(me + i, count)
            body(other // nb, lax.rem(other, nb))
            return carry

        lax.fori_loop(1, count, run, 0)

    others(lambda go, bo: pl.semaphore_signal(
        barrier, inc=1, device_id=(go, bo), device_id_type=pl.DeviceIdType.MESH))

    def halo_copies(ref, level, h, slot):
        for index, (dx, dy) in enumerate(DIRECTIONS):
            n, m = level.nx, level.ny
            sx, tx_, wx = {-1: (HX, HX + n, h), 0: (HX, HX, n), 1: (HX + n - h, HX - h, h)}[dx]
            sy, ty_, wy = {-1: (YO, YO + m, 8), 0: (YO, YO, m), 1: (YO + m - 8, YO - 8, 8)}[dy]
            to_g, to_b, from_g, from_b = g + dx, b + dy, g - dx, b - dy
            sends = (to_g >= 0) & (to_g < ng) & (to_b >= 0) & (to_b < nb)
            receives = (from_g >= 0) & (from_g < ng) & (from_b >= 0) & (from_b < nb)
            copy = pltpu.make_async_remote_copy(
                src_ref=ref.at[pl.ds(sx, wx), pl.ds(sy, wy), :],
                dst_ref=ref.at[pl.ds(tx_, wx), pl.ds(ty_, wy), :],
                send_sem=halo_send.at[slot, index],
                recv_sem=halo_recv.at[slot, index],
                device_id=(to_g, to_b),
                device_id_type=pl.DeviceIdType.MESH,
            )
            yield sends, receives, copy

    def halo_start(*args):
        for sends, _, copy in halo_copies(*args):
            pl.when(sends)(copy.start)

    def halo_wait(*args):
        for _, receives, copy in halo_copies(*args):
            pl.when(receives)(copy.wait_recv)

    def halo_sent(*args):
        for sends, _, copy in halo_copies(*args):
            pl.when(sends)(copy.wait_send)

    def gather_start(which):
        mine = slots[which].at[me]

        def body(go, bo):
            pltpu.make_async_remote_copy(
                src_ref=mine,
                dst_ref=mine,
                send_sem=all_send.at[which],
                recv_sem=all_recv.at[which],
                device_id=(go, bo),
                device_id_type=pl.DeviceIdType.MESH,
            ).start()

        others(body)

    def gather_wait(which, sem):
        part = slots[which].at[pl.ds(0, count - 1)]
        pltpu.make_async_copy(part, part, sem.at[which]).wait()

    def fill(x, _):
        for y in tiles(0, ny):
            tag = tags[x, pl.ds(y, 8), :]
            value = jnp.full(tag.shape, coef[0], jnp.float32)
            for region in range(1, coef.shape[0]):
                value = jnp.where(tag == region, coef[region], value)
            L[0].C[HX + x, pl.ds(YO + y, 8), :] = value * rough[x, pl.ds(y, 8), :] * 0.5
            f0[HX + x, pl.ds(YO + y, 8), :] = source[x, pl.ds(y, 8), :]

    each_x(0, nx, 1, fill)
    coef_pairs(L[0], R0)
    coarse_rows(L[0], R0, 0.125, L[1].C, HX, YO)
    coef_pairs(L[1], R1)
    coarse_rows(L[1], R1, 0.125, L[2].C, HX, YO)
    coef_pairs(L[2], R2)
    slots[0][me] = packed(L[2], R2, 0.125)

    pl.semaphore_wait(barrier, count - 1)
    start = [(L[0].C, L[0], 7, 0), (f0, L[0], 6, 1), (L[1].C, L[1], 7, 2), (L[2].C, L[2], 7, 3)]
    for args in start:
        halo_start(*args)
    gather_start(0)
    halo_wait(*start[0])
    operators(L[0], 6)
    halo_wait(*start[1])
    first_sweep(L[0], f0, L[0].VA, 6)
    sweep(L[0], f0, L[0].VA, L[0].VB, 5)
    sent = list(start)

    for cycle in range(2):
        wide = 6 if cycle == 0 else 4
        if cycle == 1:
            sweep(L[0], f0, L[0].VB, L[0].VA, 2)
            sweep(L[0], f0, L[0].VA, L[0].VB, 1)
        residual_pairs(L[0], f0, L[0].VB, R0)
        coarse_rows(L[0], R0, 0.5, f1[cycle], HX, YO)
        args = (f1[cycle], L[1], 6, 4 + cycle)
        halo_start(*args)
        sent.append(args)
        if cycle == 1:
            def keep(x, _):
                at = (x, pl.ds(YO, ny), slice(None))
                kept[at] = L[0].VB[at]

            each_x(HX, nx, 1, keep)
            kept_args = (kept, L[0], 3, 8)
            halo_start(*kept_args)
            sent.append(kept_args)
        if cycle == 0:
            halo_wait(*start[2])
            operators(L[1], 6)
        halo_wait(*args)
        first_sweep(L[1], f1[cycle], L[1].VA, 6)
        sweep(L[1], f1[cycle], L[1].VA, L[1].VB, 5)
        residual_pairs(L[1], f1[cycle], L[1].VB, R1)
        coarse_rows(L[1], R1, 0.5, f2[cycle], HX, YO)
        args = (f2[cycle], L[2], 6, 6 + cycle)
        halo_start(*args)
        sent.append(args)
        if cycle == 0:
            halo_wait(*start[3])
            operators(L[2], 6)
        halo_wait(*args)
        first_sweep(L[2], f2[cycle], L[2].VA, 6)
        sweep(L[2], f2[cycle], L[2].VA, L[2].VB, 5)
        residual_pairs(L[2], f2[cycle], L[2].VB, R2)
        slots[1 + cycle][me] = packed(L[2], R2, 0.5)
        gather_start(1 + cycle)
        if cycle == 0:
            gather_wait(0, all_recv)
            unpack(slots[0], flat, L[3].C, ng, nb, tx, ty)
            operators(L[3], 0)
            coef_pairs(L[3], R3)
            coarse_rows(L[3], R3, 0.125, L[4].C, 2, GY)
            operators(L[4], 0)
        gather_wait(1 + cycle, all_recv)
        unpack(slots[1 + cycle], flat, f3, ng, nb, tx, ty)
        first_sweep(L[3], f3, L[3].VA, 0)
        sweep(L[3], f3, L[3].VA, L[3].VB, 0)
        residual_pairs(L[3], f3, L[3].VB, R3)
        coarse_rows(L[3], R3, 0.5, f4, 2, GY)
        krylov(L[4], f4, L[4].VB, L[4].VA)
        add_refined(L[3], L[3].VB, L[3].VB, L[4].VB, 2, GY, 0)
        sweep(L[3], f3, L[3].VB, L[3].VA, 0)
        sweep(L[3], f3, L[3].VA, L[3].VB, 0)
        add_refined(L[2], L[2].VB, L[2].VB, L[3].VB, GX + g * tx - wide // 2,
                    pl.multiple_of(GY - 4 + b * ty, 4), wide)
        sweep(L[2], f2[cycle], L[2].VB, L[2].VA, wide // 2 + 1)
        sweep(L[2], f2[cycle], L[2].VA, L[2].VB, wide // 2)
        add_refined(L[1], L[1].VB, L[1].VB, L[2].VB, HX - wide // 2, YO - 4, wide)
        sweep(L[1], f1[cycle], L[1].VB, L[1].VA, wide // 2 + 1)
        sweep(L[1], f1[cycle], L[1].VA, L[1].VB, wide // 2)
        if cycle == 1:
            halo_wait(*kept_args)
        before = L[0].VB if cycle == 0 else kept
        add_refined(L[0], before, L[0].VB, L[1].VB, HX - wide // 2, YO - 4, wide)
        sweep(L[0], f0, L[0].VB, L[0].VA, wide - 2)
        sweep(L[0], f0, L[0].VA, L[0].VB, wide - 3)

    def finish(x, i):
        for y in tiles(YO, YO + ny):
            at = (pl.ds(x, 2), pl.ds(y, 8), slice(None))
            to = (pl.ds(2 * i, 2), pl.ds(y - YO, 8), slice(None))
            center, total = off_diagonal(L[0], L[0].VB, x, 2, y, 8)
            out_v[to] = center
            out_r[to] = f0[at] - L[0].D[at] * center + total

    each_x(HX, nx, 2, finish)
    for args in sent:
        halo_sent(*args)
    for which in range(3):
        gather_wait(which, all_send)


def body(ng, nb, source_field, region_tags, region_coef, roughness):
    nx, ny, nz = source_field.shape
    f32 = jnp.float32
    shapes = []
    padded = [(((nx >> l) + 2 * HX, (ny >> l) + 2 * YO, nz)) for l in range(3)]
    tx, ty = nx >> 3, ny >> 3
    padded.append((ng * tx + 2 * GX, nb * ty + 2 * GY, nz))
    padded.append((ng * tx // 2 + 4, nb * ty // 2 + 2 * GY, nz))
    for shape in padded:
        shapes += [shape] * 7
    shapes += [padded[0], padded[1], padded[1], padded[2], padded[2], padded[3], padded[4], padded[0]]
    shapes += [(nx >> (l + 1), ny >> l, nz) for l in range(3)]
    shapes += [(ng * tx // 2, nb * ty, nz), (nb * ty, nz)]
    shapes += [(ng * nb, ty, nz)] * 3
    dma = pltpu.SemaphoreType.DMA
    vmem = pl.BlockSpec(memory_space=pltpu.VMEM)
    return pl.pallas_call(
        functools.partial(kernel, ng, nb),
        out_shape=[jax.ShapeDtypeStruct(source_field.shape, f32)] * 2,
        in_specs=[vmem, vmem, pl.BlockSpec(memory_space=pltpu.SMEM), vmem],
        out_specs=[vmem, vmem],
        scratch_shapes=[pltpu.VMEM(shape, f32) for shape in shapes]
        + [dma((9, 8)), dma((9, 8)), dma((3,)), dma((3,))],
        compiler_params=pltpu.CompilerParams(
            collective_id=0, has_side_effects=True, vmem_limit_bytes=60 * 1024 * 1024
        ),
    )(source_field, region_tags, region_coef, roughness)


def solution(mesh):
    spec = P("grp", "box", None)
    return jax.shard_map(
        functools.partial(body, mesh.shape["grp"], mesh.shape["box"]),
        mesh=mesh,
        in_specs=(spec, spec, P(), spec),
        out_specs=(spec, spec),
        check_vma=False,
    )
```

time: 1500 us -> 118 us (0.08)
  starting transfers between devices: 439 us -> 0 us
  local copies, waits for them, and re-layouts: 331 us -> 2.72 us
  other arithmetic: 300 us -> 0 us
  waiting for transfers between devices: 206 us -> 0 us
  blocking collectives: 191 us -> 0 us
  Pallas kernels: 0 us -> 114 us
  between operations: 23.8 us -> 0.65 us
    ppermute x186 -> x0, starting transfers between devices: 439 us -> none  [the longest x93 316 us: padded_2(): before = lax.ppermute(last, axis, up)]
    ppermute x186 -> x0, waiting for transfers between devices: 206 us -> none  [the longest x93 203 us: padded_2(): after = lax.ppermute(first, axis, down)]
    reshape x23 -> x0, local copies, waits for them, and re-layouts: 130 us -> none  [the longest x9 120 us: coarsen(): values.reshape(size_x // 2, 2, size_y // 2, 2, size_z // 2, 2)]
    pallas_call x0 -> x1, Pallas kernels: none -> 114 us  [body(): pl.pallas_call(functools.partial(kernel, ng, nb), out_shape=[jax.ShapeDty...]
    psum x14 -> x0, blocking collectives: 107 us -> none  [group_total(): return lax.psum(value, 'grp')]
    slice x84 -> x0, local copies, waits for them, and re-layouts: 101 us -> none  [the longest x70 69.9 us: padded_2(): last = lax.slice_in_dim(x, length - width, length, axis=dim)]
    add x41 -> x0, other arithmetic: 93.7 us -> none  [the longest x25 88.1 us: smooth(): values = values + relax_weight * (source - result) / diag_sum]
    concatenate x93 -> x0, other arithmetic: 84.2 us -> none  [padded_2(): x = jnp.concatenate([before, x, after], axis=dim)]
  transfers between devices with their start and end apart: 186 -> 0, of which waited for: 74 -> 0; matrix products, arithmetic and copies ran while one was open for 20% -> 0% of each run, Pallas kernels for 0% -> 0%
where the time goes in v1:
time: 118 us
  Pallas kernels  114 us (97%)
  local copies, waits for them, and re-layouts  2.72 us (2%)
    pallas_call x1, Pallas kernels, body(): pl.pallas_call(functools.partial(kernel, ng, nb), out_shape=[jax.ShapeDty...  114 us
    unnamed x4, local copies, waits for them, and re-layouts  2.72 us

profile of v1, /device:TPU:0, one launch (start us, length us, event | category | flops | bytes accessed | tf_op | source)
XLA Modules:
  0.0 117.5 jit_solution(18266585920877658487)
XLA Ops:
  0.6 114.2 %shard_map.59 = (f32[32,32,128]{2,1,0:T(8,128)}, f32[32,32,128]{2,1,0:T(8,128)}) custom-call(f32[32,32,128]{2,1,0:T(8,128)} %source.1, s32[32,32,128]{2,1,0:T(8,128)} %tags.1, f32[8]{0:T(128)} %coef.1, f32[32,32,128]{2,1,0:T(8,128)} %rough.1), custom_call_target="tpu_custom_call" | custom-call | tf_op jit(solution)/shard_map/pallas_call | solution.py:432
  114.8 0.0 copy-start
  114.8 1.9 %copy.8 = f32[32,32,128]{2,1,0:T(8,128)} copy(f32[32,32,128]{2,1,0:T(8,128)} %get-tuple-element.4) | data formatting | bytes 1048576
  116.7 0.0 copy-done
  116.7 0.8 copy.9
Async XLA Ops:
  114.8 1.9 %copy-start = (f32[32,32,128]{2,1,0:T(8,128)S(1)}, f32[32,32,128]{2,1,0:T(8,128)}, u32[]{:S(2)}) copy-start(f32[32,32,128]{2,1,0:T(8,128)} %get-tuple-element.5) | copy-start | bytes 1572868

commit v2 on v1

--- a/solution.py
+++ b/solution.py
@@ -16,10 +16,11 @@
 
 
 class Level:
-    def __init__(self, shift, nx, ny, x0, y0, ylo, yhi, refs):
+    def __init__(self, shift, nx, ny, x0, y0, ylo, yhi, step, zero, refs):
         self.shift, self.nx, self.ny, self.x0, self.y0 = shift, nx, ny, x0, y0
-        self.ylo, self.yhi = ylo, yhi
-        self.C, self.WL, self.WH, self.G, self.D, self.VA, self.VB = refs
+        self.ylo, self.yhi, self.step, self.zero = ylo, yhi, step, zero
+        self.WX, self.WY, self.WZ, self.G, self.D, self.VA, self.VB = refs[:7]
+        self.C = refs[7] if len(refs) > 7 else self.VA
 
 
 def lane_index(shape):
@@ -36,18 +37,17 @@
 
 
 def off_diagonal(L, V, x, n, y, rows):
+    down, up = y - 1 + L.zero, y + 1 + L.zero
     block = V[pl.ds(x - 1, n + 2), pl.ds(y, rows), :]
-    coef = L.C[pl.ds(x - 1, n + 2), pl.ds(y, rows), :]
-    flow = block * coef
-    center, near = block[1:-1], coef[1:-1]
-    v_down = V[pl.ds(x, n), pl.ds(y - 1, rows), :]
-    v_up = V[pl.ds(x, n), pl.ds(y + 1, rows), :]
-    c_down = L.C[pl.ds(x, n), pl.ds(y - 1, rows), :]
-    c_up = L.C[pl.ds(x, n), pl.ds(y + 1, rows), :]
-    total = (block[:-2] + block[2:]) + (v_down + v_up)
-    total = near * total + (flow[:-2] + flow[2:]) + (c_down * v_down + c_up * v_up)
-    total = total + L.WL[pl.ds(x, n), pl.ds(y, rows), :] * roll(center, L.shift)
-    total = total + L.WH[pl.ds(x, n), pl.ds(y, rows), :] * roll(center, LANES - L.shift)
+    center = block[1:-1]
+    wx = L.WX[pl.ds(x, n + 1), pl.ds(y, rows), :]
+    wz = L.WZ[pl.ds(x, n), pl.ds(y, rows), :]
+    total = wz * roll(center, L.shift) + roll(wz * center, LANES - L.shift)
+    total = total + (wx[:-1] * block[:-2] + wx[1:] * block[2:])
+    total = total + (
+        L.WY[pl.ds(x, n), pl.ds(y, rows), :] * V[pl.ds(x, n), pl.ds(down, rows), :]
+        + L.WY[pl.ds(x, n), pl.ds(up, rows), :] * V[pl.ds(x, n), pl.ds(up, rows), :]
+    )
     return center, total
 
 
@@ -63,62 +63,102 @@
     return range(lo, hi, 8)
 
 
+def store_all(stores):
+    for ref, at, value in stores:
+        ref[at] = value
+
+
+def halo_range(L, k):
+    count = -(-(L.nx + 2 * k) // L.step) * L.step
+    return L.x0 - (count - L.nx) // 2, count
+
+
 def operators(L, k):
+    n = L.step
+
     def body(x, i):
+        stores = []
         for y in tiles(L.ylo, L.yhi):
-            at = (pl.ds(x, 2), pl.ds(y, 8), slice(None))
-            coef = L.C[pl.ds(x - 1, 4), pl.ds(y, 8), :]
+            at = (pl.ds(x, n), pl.ds(y, 8), slice(None))
+            coef = L.C[pl.ds(x - 1, n + 2), pl.ds(y, 8), :]
             c = coef[1:-1]
             lane = lane_index(c.shape)
-            down = jnp.where(lane < L.shift, 0.0, roll(c, L.shift))
-            up = jnp.where(lane >= LANES - L.shift, 0.0, roll(c, LANES - L.shift))
-            L.WL[at] = jnp.where(lane < L.shift, 0.0, c + down)
-            L.WH[at] = jnp.where(lane >= LANES - L.shift, 0.0, c + up)
-            diag = 6.0 * c + (coef[:-2] + coef[2:]) + (down + up)
-            diag = diag + (L.C[pl.ds(x, 2), pl.ds(y - 1, 8), :] + L.C[pl.ds(x, 2), pl.ds(y + 1, 8), :])
-            L.D[at] = diag
-            L.G[at] = jnp.where(c > 0.0, 0.8 / jnp.where(c > 0.0, diag, 1.0), 0.0)
-
-    each_x(L.x0 - k, L.nx + 2 * k, 2, body)
+            low = jnp.where(lane < L.shift, 0.0, roll(c, L.shift))
+            high = jnp.where(lane >= LANES - L.shift, 0.0, roll(c, LANES - L.shift))
+            before = L.C[pl.ds(x, n), pl.ds(y - 1 + L.zero, 8), :]
+            after = L.C[pl.ds(x, n), pl.ds(y + 1 + L.zero, 8), :]
+            diag = 6.0 * c + (coef[:-2] + coef[2:]) + (low + high) + (before + after)
+            inside = c > 0.0
+            stores += [
+                (L.WX, (pl.ds(x, n + 1), pl.ds(y, 8), slice(None)), coef[1:] + coef[:-1]),
+                (L.WY, at, c + before),
+                (L.WZ, at, jnp.where(lane < L.shift, 0.0, c + low)),
+                (L.G, at, jnp.where(inside, 0.8 / jnp.where(inside, diag, 1.0), 0.0)),
+            ]
+            if L.y0 <= y < L.y0 + L.ny:
+                stores.append((L.D, (pl.ds(x, n), pl.ds(y - L.y0, 8), slice(None)), diag))
+            if y + 8 == L.yhi:
+                last = (pl.ds(x, n), pl.ds(L.yhi, 8), slice(None))
+                stores.append((L.WY, last, L.C[last] + L.C[pl.ds(x, n), pl.ds(L.yhi - 1 + L.zero, 8), :]))
+        store_all(stores)
+
+    start, count = halo_range(L, k)
+    each_x(start, count, n, body)
 
 
 def first_sweep(L, F, dst, k):
     def body(x, i):
+        stores = []
         for y in tiles(L.ylo, L.yhi):
-            at = (pl.ds(x, 2), pl.ds(y, 8), slice(None))
-            dst[at] = L.G[at] * F[at]
-
-    each_x(L.x0 - k, L.nx + 2 * k, 2, body)
+            at = (pl.ds(x, L.step), pl.ds(y, 8), slice(None))
+            stores.append((dst, at, L.G[at] * F[at]))
+        store_all(stores)
+
+    start, count = halo_range(L, k)
+    each_x(start, count, L.step, body)
 
 
 def sweep(L, F, src, dst, k):
     def body(x, i):
+        stores = []
         for y in tiles(L.ylo, L.yhi):
-            at = (pl.ds(x, 2), pl.ds(y, 8), slice(None))
-            center, total = off_diagonal(L, src, x, 2, y, 8)
-            dst[at] = 0.2 * center + L.G[at] * (F[at] + total)
-
-    each_x(L.x0 - k, L.nx + 2 * k, 2, body)
+            at = (pl.ds(x, L.step), pl.ds(y, 8), slice(None))
+            center, total = off_diagonal(L, src, x, L.step, y, 8)
+            stores.append((dst, at, 0.2 * center + L.G[at] * (F[at] + total)))
+        store_all(stores)
+
+    start, count = halo_range(L, k)
+    each_x(start, count, L.step, body)
 
 
 def residual_pairs(L, F, V, R):
+    n = L.step
+
+    def body(x, i):
+        stores = []
+        for y in tiles(L.y0, L.y0 + L.ny):
+            at = (pl.ds(x, n), pl.ds(y, 8), slice(None))
+            center, total = off_diagonal(L, V, x, n, y, 8)
+            diag = L.D[pl.ds(x, n), pl.ds(y - L.y0, 8), :]
+            left = F[at] - diag * center + total
+            for p in range(n // 2):
+                stores.append((R, (i * (n // 2) + p, pl.ds(y - L.y0, 8), slice(None)),
+                               left[2 * p] + left[2 * p + 1]))
+        store_all(stores)
+
+    each_x(L.x0, L.nx, n, body)
+
+
+def coef_pairs(L, R):
+    n = L.step
+
     def body(x, i):
         for y in tiles(L.y0, L.y0 + L.ny):
-            at = (pl.ds(x, 2), pl.ds(y, 8), slice(None))
-            center, total = off_diagonal(L, V, x, 2, y, 8)
-            left = F[at] - L.D[at] * center + total
-            R[i, pl.ds(y - L.y0, 8), :] = left[0] + left[1]
-
-    each_x(L.x0, L.nx, 2, body)
-
-
-def coef_pairs(L, R):
-    def body(x, i):
-        for y in tiles(L.y0, L.y0 + L.ny):
-            c = L.C[pl.ds(x, 2), pl.ds(y, 8), :]
-            R[i, pl.ds(y - L.y0, 8), :] = c[0] + c[1]
-
-    each_x(L.x0, L.nx, 2, body)
+            c = L.C[pl.ds(x, n), pl.ds(y, 8), :]
+            for p in range(n // 2):
+                R[i * (n // 2) + p, pl.ds(y - L.y0, 8), :] = c[2 * p] + c[2 * p + 1]
+
+    each_x(L.x0, L.nx, n, body)
 
 
 def coarse_row(L, R, i, factor):
@@ -128,10 +168,15 @@
 
 
 def coarse_rows(L, R, factor, dst, x0, y0):
+    count = L.nx // 2
+    n = 8 if count % 8 == 0 else 4
+
     def body(i, _):
-        dst[x0 + i, pl.ds(y0, L.ny // 2), :] = coarse_row(L, R, i, factor)
-
-    each_x(0, L.nx // 2, 1, body)
+        rows = [coarse_row(L, R, i + p, factor) for p in range(n)]
+        for p in range(n):
+            dst[x0 + i + p, pl.ds(y0, L.ny // 2), :] = rows[p]
+
+    each_x(0, count, n, body)
 
 
 def packed(L, R, factor):
@@ -145,11 +190,13 @@
 
 
 def unpack(slots, flat, dst, ng, nb, tx, ty):
+    def gather(g, _):
+        for b in range(nb):
+            flat[g, pl.ds(b * ty, ty), :] = slots[g * nb + b]
+
     def body(g, _):
-        for b in range(nb):
-            flat[pl.ds(b * ty, ty), :] = slots[g * nb + b]
         for y in tiles(0, nb * ty):
-            rows = flat[pl.ds(y, 8), :]
+            rows = flat[g, pl.ds(y, 8), :]
             rolled = {d: roll(rows, d) for d in range(1 - tx, tx)}
             which = lane_index(rows.shape) % tx
             for i in range(tx):
@@ -158,6 +205,7 @@
                     out = jnp.where(which == d, rolled[d - i], out)
                 dst[GX + g * tx + i, pl.ds(GY + y, 8), :] = out
 
+    each_x(0, ng, 1, gather)
     each_x(0, ng, 1, body)
 
 
@@ -165,13 +213,16 @@
     half = (L.yhi - L.ylo) // 2
 
     def body(x, i):
-        e = E[ex + i, pl.ds(ey, half), :]
-        for dx in range(2):
-            for phase in range(2):
-                at = (x + dx, pl.ds(L.ylo + phase, half, stride=2), slice(None))
-                dst[at] = src[at] + e
-
-    each_x(L.x0 - k, L.nx + 2 * k, 2, body)
+        stores = []
+        for p in range(2):
+            e = E[ex + 2 * i + p, pl.ds(ey, half), :]
+            for dx in range(2):
+                for phase in range(2):
+                    at = (x + 2 * p + dx, pl.ds(L.ylo + phase, half, stride=2), slice(None))
+                    stores.append((dst, at, src[at] + e))
+        store_all(stores)
+
+    each_x(L.x0 - k, L.nx + 2 * k, 4, body)
 
 
 def total_of(values):
@@ -187,7 +238,7 @@
     for step in range(NB):
         V[at] = direction
         _, total = off_diagonal(L, V, L.x0, L.nx, L.y0, L.ny)
-        image = L.D[at] * direction - total
+        image = L.D[pl.ds(L.x0, L.nx)] * direction - total
         alpha = norm_now / total_of(direction * image)
         values = values + alpha * direction
         if step < NB - 1:
@@ -205,6 +256,22 @@
     each_x(0, ref.shape[0], 1, body)
 
 
+def zero_halo(ref, L, k):
+    y0, y1, nx = L.y0, L.y0 + L.ny, L.nx
+
+    def ends(i, _):
+        rows = jnp.zeros((y1 - y0 + 16, LANES), ref.dtype)
+        ref[HX - k + i, pl.ds(y0 - 8, y1 - y0 + 16), :] = rows
+        ref[HX + nx + i, pl.ds(y0 - 8, y1 - y0 + 16), :] = rows
+
+    def sides(x, _):
+        ref[x, pl.ds(y0 - 8, 8), :] = jnp.zeros((8, LANES), ref.dtype)
+        ref[x, pl.ds(y1, 8), :] = jnp.zeros((8, LANES), ref.dtype)
+
+    each_x(0, k, 1, ends)
+    each_x(HX, nx, 1, sides)
+
+
 def kernel(ng, nb, source, tags, coef, rough, out_v, out_r, *scratch):
     scratch = list(scratch)
 
@@ -213,29 +280,29 @@
         del scratch[:count]
         return taken
 
+    g, b = lax.axis_index("grp"), lax.axis_index("box")
+    me = g * nb + b
+    count = ng * nb
+    none = lax.div(g, jnp.int32(ng))
+
     nx, ny = source.shape[0], source.shape[1]
     L = []
     for l in range(3):
-        L.append(Level(1 << l, nx >> l, ny >> l, HX, YO, 8, (ny >> l) + 24, take(7)))
+        L.append(Level(1 << l, nx >> l, ny >> l, HX, YO, 8, (ny >> l) + 24, 4, none, take(8)))
     tx, ty = nx >> 3, ny >> 3
-    L.append(Level(8, ng * tx, nb * ty, GX, GY, GY, GY + nb * ty, take(7)))
-    L.append(Level(16, ng * tx // 2, nb * ty // 2, 2, GY, GY, GY + nb * ty // 2, take(7)))
+    L.append(Level(8, ng * tx, nb * ty, GX, GY, GY, GY + nb * ty, 4 if nb * ty <= 32 else 2, none, take(7)))
+    L.append(Level(16, ng * tx // 2, nb * ty // 2, 2, GY, GY, GY + nb * ty // 2, ng * tx // 2, none, take(7)))
     f0, f1a, f1b, f2a, f2b, f3, f4, kept = take(8)
     f1, f2 = (f1a, f1b), (f2a, f2b)
-    R0, R1, R2, R3, flat = take(5)
+    R0, R3 = take(2)
+    R1 = R2 = R0
+    flat = R3
     slots = take(3)
     halo_send, halo_recv, all_send, all_recv = take(4)
 
-    g, b = lax.axis_index("grp"), lax.axis_index("box")
-    me = g * nb + b
-    count = ng * nb
-
-    for ref in [f0, f1a, f1b, f2a, f2b, kept]:
-        zero(ref)
-    for level in L:
-        zero(level.C)
-        zero(level.VA)
-        zero(level.VB)
+    for ref, level in [(L[0].C, L[0]), (f0, L[0]), (kept, L[0]), (L[1].C, L[1]), (f1a, L[1]),
+                       (f1b, L[1]), (L[2].C, L[2]), (f2a, L[2]), (f2b, L[2])]:
+        zero_halo(ref, level, 7)
 
     barrier = pltpu.get_barrier_semaphore()
 
@@ -250,7 +317,7 @@
     others(lambda go, bo: pl.semaphore_signal(
         barrier, inc=1, device_id=(go, bo), device_id_type=pl.DeviceIdType.MESH))
 
-    def halo_copies(ref, level, h, slot):
+    def halo_copies(ref, level, h, slot, src=None):
         for index, (dx, dy) in enumerate(DIRECTIONS):
             n, m = level.nx, level.ny
             sx, tx_, wx = {-1: (HX, HX + n, h), 0: (HX, HX, n), 1: (HX + n - h, HX - h, h)}[dx]
@@ -258,8 +325,9 @@
             to_g, to_b, from_g, from_b = g + dx, b + dy, g - dx, b - dy
             sends = (to_g >= 0) & (to_g < ng) & (to_b >= 0) & (to_b < nb)
             receives = (from_g >= 0) & (from_g < ng) & (from_b >= 0) & (from_b < nb)
+            lead, side = (0, 0) if src is None else (HX, YO)
             copy = pltpu.make_async_remote_copy(
-                src_ref=ref.at[pl.ds(sx, wx), pl.ds(sy, wy), :],
+                src_ref=(ref if src is None else src).at[pl.ds(sx - lead, wx), pl.ds(sy - side, wy), :],
                 dst_ref=ref.at[pl.ds(tx_, wx), pl.ds(ty_, wy), :],
                 send_sem=halo_send.at[slot, index],
                 recv_sem=halo_recv.at[slot, index],
@@ -300,26 +368,34 @@
         pltpu.make_async_copy(part, part, sem.at[which]).wait()
 
     def fill(x, _):
-        for y in tiles(0, ny):
-            tag = tags[x, pl.ds(y, 8), :]
-            value = jnp.full(tag.shape, coef[0], jnp.float32)
-            for region in range(1, coef.shape[0]):
-                value = jnp.where(tag == region, coef[region], value)
-            L[0].C[HX + x, pl.ds(YO + y, 8), :] = value * rough[x, pl.ds(y, 8), :] * 0.5
-            f0[HX + x, pl.ds(YO + y, 8), :] = source[x, pl.ds(y, 8), :]
-
-    each_x(0, nx, 1, fill)
+        stores = []
+        for dx in range(2):
+            for y in tiles(0, ny):
+                tag = tags[x + dx, pl.ds(y, 8), :]
+                value = jnp.full(tag.shape, coef[0], jnp.float32)
+                for region in range(1, coef.shape[0]):
+                    value = jnp.where(tag == region, coef[region], value)
+                at = (HX + x + dx, pl.ds(YO + y, 8), slice(None))
+                stores.append((L[0].C, at, value * rough[x + dx, pl.ds(y, 8), :] * 0.5))
+                stores.append((f0, at, source[x + dx, pl.ds(y, 8), :]))
+        store_all(stores)
+
+    each_x(0, nx, 2, fill)
+    pl.semaphore_wait(barrier, count - 1)
+    start = [(L[0].C, L[0], 7, 0), (f0, L[0], 6, 1, source), (L[1].C, L[1], 7, 2), (L[2].C, L[2], 7, 3)]
+    halo_start(*start[0])
+    halo_start(*start[1])
+    for level in L[3:]:
+        zero(level.VA)
+        zero(level.VB)
     coef_pairs(L[0], R0)
     coarse_rows(L[0], R0, 0.125, L[1].C, HX, YO)
     coef_pairs(L[1], R1)
     coarse_rows(L[1], R1, 0.125, L[2].C, HX, YO)
     coef_pairs(L[2], R2)
     slots[0][me] = packed(L[2], R2, 0.125)
-
-    pl.semaphore_wait(barrier, count - 1)
-    start = [(L[0].C, L[0], 7, 0), (f0, L[0], 6, 1), (L[1].C, L[1], 7, 2), (L[2].C, L[2], 7, 3)]
-    for args in start:
-        halo_start(*args)
+    halo_start(*start[2])
+    halo_start(*start[3])
     gather_start(0)
     halo_wait(*start[0])
     operators(L[0], 6)
@@ -404,7 +480,7 @@
             to = (pl.ds(2 * i, 2), pl.ds(y - YO, 8), slice(None))
             center, total = off_diagonal(L[0], L[0].VB, x, 2, y, 8)
             out_v[to] = center
-            out_r[to] = f0[at] - L[0].D[at] * center + total
+            out_r[to] = f0[at] - L[0].D[pl.ds(x, 2), pl.ds(y - YO, 8), :] * center + total
 
     each_x(HX, nx, 2, finish)
     for args in sent:
@@ -421,11 +497,11 @@
     tx, ty = nx >> 3, ny >> 3
     padded.append((ng * tx + 2 * GX, nb * ty + 2 * GY, nz))
     padded.append((ng * tx // 2 + 4, nb * ty // 2 + 2 * GY, nz))
-    for shape in padded:
-        shapes += [shape] * 7
+    for index, shape in enumerate(padded):
+        own = (shape[0], shape[1] - 2 * (YO if index < 3 else GY), nz)
+        shapes += [shape] * 4 + [own] + [shape] * (3 if index < 3 else 2)
     shapes += [padded[0], padded[1], padded[1], padded[2], padded[2], padded[3], padded[4], padded[0]]
-    shapes += [(nx >> (l + 1), ny >> l, nz) for l in range(3)]
-    shapes += [(ng * tx // 2, nb * ty, nz), (nb * ty, nz)]
+    shapes += [(nx // 2, ny, nz), (ng * tx // 2, nb * ty, nz)]
     shapes += [(ng * nb, ty, nz)] * 3
     dma = pltpu.SemaphoreType.DMA
     vmem = pl.BlockSpec(memory_space=pltpu.VMEM)
@@ -437,7 +513,7 @@
         scratch_shapes=[pltpu.VMEM(shape, f32) for shape in shapes]
         + [dma((9, 8)), dma((9, 8)), dma((3,)), dma((3,))],
         compiler_params=pltpu.CompilerParams(
-            collective_id=0, has_side_effects=True, vmem_limit_bytes=60 * 1024 * 1024
+            collective_id=0, has_side_effects=True, vmem_limit_bytes=63 * 1024 * 1024
         ),
     )(source_field, region_tags, region_coef, roughness)
 

time: 118 us -> 99.1 us (0.84)
  Pallas kernels: 114 us -> 95.6 us
    pallas_call x1, Pallas kernels: 114 us -> 95.6 us  [body(): pl.pallas_call(functools.partial(kernel, ng, nb), out_shape=[jax.ShapeDty...]
where the time goes in v2:
time: 99.1 us; the launch traced here: 99 us
  Pallas kernels  95.6 us (96%)
  local copies, waits for them, and re-layouts  2.72 us (3%)
    pallas_call x1, Pallas kernels, body(): pl.pallas_call(functools.partial(kernel, ng, nb), out_shape=[jax.ShapeDty...  95.6 us
    unnamed x4, local copies, waits for them, and re-layouts  2.72 us

profile of v2, /device:TPU:0, one launch (start us, length us, event | category | flops | bytes accessed | tf_op | source)
XLA Modules:
  0.0 99.0 jit_solution(16049570795106599516)
XLA Ops:
  0.6 95.6 %shard_map.59 = (f32[32,32,128]{2,1,0:T(8,128)}, f32[32,32,128]{2,1,0:T(8,128)}) custom-call(f32[32,32,128]{2,1,0:T(8,128)} %source.1, s32[32,32,128]{2,1,0:T(8,128)} %tags.1, f32[8]{0:T(128)} %coef.1, f32[32,32,128]{2,1,0:T(8,128)} %rough.1), custom_call_target="tpu_custom_call" | custom-call | tf_op jit(solution)/shard_map/pallas_call | solution.py:508
  96.2 0.0 copy-start
  96.2 1.9 %copy.8 = f32[32,32,128]{2,1,0:T(8,128)} copy(f32[32,32,128]{2,1,0:T(8,128)} %get-tuple-element.4) | data formatting | bytes 1048576
  98.2 0.0 copy-done
  98.2 0.8 copy.9
Async XLA Ops:
  96.2 1.9 %copy-start = (f32[32,32,128]{2,1,0:T(8,128)S(1)}, f32[32,32,128]{2,1,0:T(8,128)}, u32[]{:S(2)}) copy-start(f32[32,32,128]{2,1,0:T(8,128)} %get-tuple-element.5) | copy-start | bytes 1572868

commit v3 on v2

--- a/solution.py
+++ b/solution.py
@@ -32,7 +32,7 @@
 
 
 def pair_sum(values, shift):
-    even = (lane_index(values.shape) // shift) % 2 == 0
+    even = (lane_index(values.shape) & shift) == 0
     return values + jnp.where(even, roll(values, LANES - shift), roll(values, shift))
 
 
@@ -182,7 +182,7 @@
 def packed(L, R, factor):
     count = L.nx // 2
     rows = [coarse_row(L, R, i, factor) for i in range(count)]
-    which = lane_index(rows[0].shape) % count
+    which = lane_index(rows[0].shape) & (count - 1)
     out = rows[0]
     for i in range(1, count):
         out = jnp.where(which == i, rows[i], out)
@@ -198,7 +198,7 @@
         for y in tiles(0, nb * ty):
             rows = flat[g, pl.ds(y, 8), :]
             rolled = {d: roll(rows, d) for d in range(1 - tx, tx)}
-            which = lane_index(rows.shape) % tx
+            which = lane_index(rows.shape) & (tx - 1)
             for i in range(tx):
                 out = rolled[-i]
                 for d in range(1, tx):
@@ -256,20 +256,24 @@
     each_x(0, ref.shape[0], 1, body)
 
 
-def zero_halo(ref, L, k):
+def zero_halo(ref, L, k, edges):
     y0, y1, nx = L.y0, L.y0 + L.ny, L.nx
 
-    def ends(i, _):
-        rows = jnp.zeros((y1 - y0 + 16, LANES), ref.dtype)
-        ref[HX - k + i, pl.ds(y0 - 8, y1 - y0 + 16), :] = rows
-        ref[HX + nx + i, pl.ds(y0 - 8, y1 - y0 + 16), :] = rows
-
-    def sides(x, _):
-        ref[x, pl.ds(y0 - 8, 8), :] = jnp.zeros((8, LANES), ref.dtype)
-        ref[x, pl.ds(y1, 8), :] = jnp.zeros((8, LANES), ref.dtype)
-
-    each_x(0, k, 1, ends)
-    each_x(HX, nx, 1, sides)
+    def ends(start):
+        for i in range(k):
+            ref[start + i, pl.ds(y0 - 8, L.ny + 16), :] = jnp.zeros((L.ny + 16, LANES), ref.dtype)
+
+    def side(y):
+        def rows(x, _):
+            ref[pl.ds(x, 8), pl.ds(y, 8), :] = jnp.zeros((8, 8, LANES), ref.dtype)
+
+        each_x(0, ref.shape[0], 8, rows)
+
+    first_x, last_x, first_y, last_y = edges
+    pl.when(first_x)(lambda: ends(HX - k))
+    pl.when(last_x)(lambda: ends(HX + nx))
+    pl.when(first_y)(lambda: side(y0 - 8))
+    pl.when(last_y)(lambda: side(y1))
 
 
 def kernel(ng, nb, source, tags, coef, rough, out_v, out_r, *scratch):
@@ -300,19 +304,20 @@
     slots = take(3)
     halo_send, halo_recv, all_send, all_recv = take(4)
 
-    for ref, level in [(L[0].C, L[0]), (f0, L[0]), (kept, L[0]), (L[1].C, L[1]), (f1a, L[1]),
-                       (f1b, L[1]), (L[2].C, L[2]), (f2a, L[2]), (f2b, L[2])]:
-        zero_halo(ref, level, 7)
+    edges = (g == 0, g == ng - 1, b == 0, b == nb - 1)
+    for ref, level in [(L[0].C, L[0]), (f0, L[0]), (L[1].C, L[1]), (L[2].C, L[2])]:
+        zero_halo(ref, level, 7, edges)
 
     barrier = pltpu.get_barrier_semaphore()
 
+    all_g = [g] + [lax.rem(g + i, ng) for i in range(1, ng)]
+    all_b = [b] + [lax.rem(b + i, nb) for i in range(1, nb)]
+
     def others(body):
-        def run(i, carry):
-            other = lax.rem(me + i, count)
-            body(other // nb, lax.rem(other, nb))
-            return carry
-
-        lax.fori_loop(1, count, run, 0)
+        for i in range(ng):
+            for j in range(nb):
+                if i or j:
+                    body(all_g[i], all_b[j])
 
     others(lambda go, bo: pl.semaphore_signal(
         barrier, inc=1, device_id=(go, bo), device_id_type=pl.DeviceIdType.MESH))
@@ -380,6 +385,8 @@
                 stores.append((f0, at, source[x + dx, pl.ds(y, 8), :]))
         store_all(stores)
 
+    for ref, level in [(f1a, L[1]), (f1b, L[1]), (f2a, L[2]), (f2b, L[2]), (kept, L[0])]:
+        zero_halo(ref, level, 7, edges)
     each_x(0, nx, 2, fill)
     pl.semaphore_wait(barrier, count - 1)
     start = [(L[0].C, L[0], 7, 0), (f0, L[0], 6, 1, source), (L[1].C, L[1], 7, 2), (L[2].C, L[2], 7, 3)]

time: 99.1 us -> 97.7 us (0.986)
  Pallas kernels: 95.6 us -> 94.2 us
    pallas_call x1, Pallas kernels: 95.6 us -> 94.2 us  [body(): pl.pallas_call(functools.partial(kernel, ng, nb), out_shape=[jax.ShapeDty...]
where the time goes in v3:
time: 97.7 us; the launch traced here: 97.5 us
  Pallas kernels  94.2 us (96%)
  local copies, waits for them, and re-layouts  2.72 us (3%)
    pallas_call x1, Pallas kernels, body(): pl.pallas_call(functools.partial(kernel, ng, nb), out_shape=[jax.ShapeDty...  94.2 us
    unnamed x4, local copies, waits for them, and re-layouts  2.72 us

profile of v3, /device:TPU:0, one launch (start us, length us, event | category | flops | bytes accessed | tf_op | source)
XLA Modules:
  0.0 97.5 jit_solution(12677183635647667409)
XLA Ops:
  0.6 94.2 %shard_map.59 = (f32[32,32,128]{2,1,0:T(8,128)}, f32[32,32,128]{2,1,0:T(8,128)}) custom-call(f32[32,32,128]{2,1,0:T(8,128)} %source.1, s32[32,32,128]{2,1,0:T(8,128)} %tags.1, f32[8]{0:T(128)} %coef.1, f32[32,32,128]{2,1,0:T(8,128)} %rough.1), custom_call_target="tpu_custom_call" | custom-call | tf_op jit(solution)/shard_map/pallas_call | solution.py:515
  94.8 0.0 copy-start
  94.8 1.9 %copy.8 = f32[32,32,128]{2,1,0:T(8,128)} copy(f32[32,32,128]{2,1,0:T(8,128)} %get-tuple-element.4) | data formatting | bytes 1048576
  96.7 0.0 copy-done
  96.7 0.8 copy.9
Async XLA Ops:
  94.8 1.9 %copy-start = (f32[32,32,128]{2,1,0:T(8,128)S(1)}, f32[32,32,128]{2,1,0:T(8,128)}, u32[]{:S(2)}) copy-start(f32[32,32,128]{2,1,0:T(8,128)} %get-tuple-element.5) | copy-start | bytes 1572868

commit v4 on v3

--- a/solution.py
+++ b/solution.py
@@ -61,6 +61,24 @@
 
 def tiles(lo, hi):
     return range(lo, hi, 8)
+
+
+def each_group(start, count, step, tiles_each, body):
+    groups = count // step
+    most = [u for u in range(1, groups + 1) if groups % u == 0 and u * tiles_each * step <= 128]
+    unroll = groups if most[-1:] in ([], [1]) and groups < 12 else max(most + [1])
+
+    def run(x, i):
+        waiting = []
+        for u in range(unroll):
+            for ref, at, value in body(x + u * step, i * unroll + u):
+                waiting.append((ref, at, value))
+                while sum(v.size for _, _, v in waiting) > 20 * 1024:
+                    store_all(waiting[:1])
+                    del waiting[:1]
+        store_all(waiting)
+
+    each_x(start, count, step * unroll, run)
 
 
 def store_all(stores):
@@ -108,45 +126,39 @@
 
 def first_sweep(L, F, dst, k):
     def body(x, i):
-        stores = []
         for y in tiles(L.ylo, L.yhi):
             at = (pl.ds(x, L.step), pl.ds(y, 8), slice(None))
-            stores.append((dst, at, L.G[at] * F[at]))
-        store_all(stores)
+            yield dst, at, L.G[at] * F[at]
 
     start, count = halo_range(L, k)
-    each_x(start, count, L.step, body)
+    each_group(start, count, L.step, (L.yhi - L.ylo) // 8, body)
 
 
 def sweep(L, F, src, dst, k):
     def body(x, i):
-        stores = []
         for y in tiles(L.ylo, L.yhi):
             at = (pl.ds(x, L.step), pl.ds(y, 8), slice(None))
             center, total = off_diagonal(L, src, x, L.step, y, 8)
-            stores.append((dst, at, 0.2 * center + L.G[at] * (F[at] + total)))
-        store_all(stores)
+            yield dst, at, 0.2 * center + L.G[at] * (F[at] + total)
 
     start, count = halo_range(L, k)
-    each_x(start, count, L.step, body)
+    each_group(start, count, L.step, (L.yhi - L.ylo) // 8, body)
 
 
 def residual_pairs(L, F, V, R):
     n = L.step
 
     def body(x, i):
-        stores = []
         for y in tiles(L.y0, L.y0 + L.ny):
             at = (pl.ds(x, n), pl.ds(y, 8), slice(None))
             center, total = off_diagonal(L, V, x, n, y, 8)
             diag = L.D[pl.ds(x, n), pl.ds(y - L.y0, 8), :]
             left = F[at] - diag * center + total
             for p in range(n // 2):
-                stores.append((R, (i * (n // 2) + p, pl.ds(y - L.y0, 8), slice(None)),
-                               left[2 * p] + left[2 * p + 1]))
-        store_all(stores)
-
-    each_x(L.x0, L.nx, n, body)
+                at = (i * (n // 2) + p, pl.ds(y - L.y0, 8), slice(None))
+                yield R, at, left[2 * p] + left[2 * p + 1]
+
+    each_group(L.x0, L.nx, n, L.ny // 8, body)
 
 
 def coef_pairs(L, R):
@@ -213,16 +225,14 @@
     half = (L.yhi - L.ylo) // 2
 
     def body(x, i):
-        stores = []
         for p in range(2):
             e = E[ex + 2 * i + p, pl.ds(ey, half), :]
             for dx in range(2):
                 for phase in range(2):
                     at = (x + 2 * p + dx, pl.ds(L.ylo + phase, half, stride=2), slice(None))
-                    stores.append((dst, at, src[at] + e))
-        store_all(stores)
-
-    each_x(L.x0 - k, L.nx + 2 * k, 4, body)
+                    yield dst, at, src[at] + e
+
+    each_group(L.x0 - k, L.nx + 2 * k, 4, half // 4, body)
 
 
 def total_of(values):

time: 97.7 us -> 88.4 us (0.905)
  Pallas kernels: 94.2 us -> 84.9 us
    pallas_call x1, Pallas kernels: 94.2 us -> 84.9 us  [body(): pl.pallas_call(functools.partial(kernel, ng, nb), out_shape=[jax.ShapeDty...]
where the time goes in v4:
time: 88.4 us; the launch traced here: 88.3 us
  Pallas kernels  84.9 us (96%)
  local copies, waits for them, and re-layouts  2.72 us (3%)
    pallas_call x1, Pallas kernels, body(): pl.pallas_call(functools.partial(kernel, ng, nb), out_shape=[jax.ShapeDty...  84.9 us
    unnamed x4, local copies, waits for them, and re-layouts  2.72 us

profile of v4, /device:TPU:0, one launch (start us, length us, event | category | flops | bytes accessed | tf_op | source)
XLA Modules:
  0.0 88.3 jit_solution(15118098652479377362)
XLA Ops:
  0.6 84.9 %shard_map.59 = (f32[32,32,128]{2,1,0:T(8,128)}, f32[32,32,128]{2,1,0:T(8,128)}) custom-call(f32[32,32,128]{2,1,0:T(8,128)} %source.1, s32[32,32,128]{2,1,0:T(8,128)} %tags.1, f32[8]{0:T(128)} %coef.1, f32[32,32,128]{2,1,0:T(8,128)} %rough.1), custom_call_target="tpu_custom_call" | custom-call | tf_op jit(solution)/shard_map/pallas_call | solution.py:525
  85.5 0.0 copy-start
  85.6 1.9 %copy.8 = f32[32,32,128]{2,1,0:T(8,128)} copy(f32[32,32,128]{2,1,0:T(8,128)} %get-tuple-element.4) | data formatting | bytes 1048576
  87.5 0.0 copy-done
  87.5 0.8 copy.9
Async XLA Ops:
  85.5 1.9 %copy-start = (f32[32,32,128]{2,1,0:T(8,128)S(1)}, f32[32,32,128]{2,1,0:T(8,128)}, u32[]{:S(2)}) copy-start(f32[32,32,128]{2,1,0:T(8,128)} %get-tuple-element.5) | copy-start | bytes 1572868
